TPU v7x, 32 devices: a whole 2x2x4 slice. The times are simulated.
32 devices in a mesh: groups: 2 (over y), seq: 4 (over z), dp: 4 (over x, core).
Axes of the slice: x: 2, y: 2, z: 4, core: 2. Of those that a mesh axis runs over, the one named last changes fastest.
Arguments:
- inputs: bfloat16 [8, 65536, 512], P(('groups', 'dp'), 'seq'), parts along dimension 0, may hold values from -6 to 6
- cotangent: bfloat16 [8, 65536, 512], P(('groups', 'dp'), 'seq'), parts along dimension 0, may hold values from -6 to 6
- first_factor: bfloat16 [256, 256, 256], P('seq', 'dp'), may hold values from -0.375 to 0.375
- second_factor: bfloat16 [256, 256, 256], P('seq', 'dp'), may hold values from -0.375 to 0.375
Outputs:
- mixed_out: bfloat16 [8, 65536, 512], P(('groups', 'dp'), 'seq'), parts along dimension 0
- input_grad: bfloat16 [8, 65536, 512], P(('groups', 'dp'), 'seq'), parts along dimension 0
- first_factor_grad: bfloat16 [512, 256, 256], P(('groups', 'seq'), 'dp'), parts along dimension 0
- second_factor_grad: bfloat16 [512, 256, 256], P(('groups', 'seq'), 'dp'), parts along dimension 0
There are 2 independent parts, one for each index of `groups`. A program takes and returns all parts, laid end to end along the dimension named above; an argument that names none is the same for every part. Nothing has to cross between parts.
All inputs are finite; a program needn't handle non-finite values.
Results may differ from a plain program's by a relative error of at most 0.009.
Values may be sent and summed in bfloat16 or wider, within the bound.
A program may use at most 320 MiB of HBM per device.

v0:
```python
import math
import jax
import jax.numpy as jnp
from jax import lax
from jax.experimental.layout import Layout, with_layout_constraint
from jax.sharding import PartitionSpec as P


def silu_parts(values):
    sig = jax.nn.sigmoid(values)
    return (values * sig, sig * (1.0 + values * (1.0 - sig)))


def row_major(value):
    return with_layout_constraint(value, Layout(tuple(range(value.ndim))))


def scatter_rows(parts):
    blocks, ring, rows, columns = parts.shape
    flat = parts.reshape(blocks, ring * rows, columns)
    kept = lax.psum_scatter(flat, "dp", scatter_dimension=1, tiled=True)
    return kept.reshape(blocks, kept.shape[1] // rows, rows, columns)


def shards(inputs, cotangent, first_factor, second_factor):
    f32, bf16 = (jnp.float32, jnp.bfloat16)
    seqs = inputs.shape[0]
    rows = inputs.shape[1]
    channels = inputs.shape[2]
    ring = lax.axis_size("seq")
    blocks = first_factor.shape[0]
    columns = second_factor.shape[0]
    width = first_factor.shape[2]
    width_two = second_factor.shape[2]
    norm_scale = 1.0 / math.sqrt(lax.axis_size("dp") * seqs * channels)
    chunks = math.gcd(4, math.gcd(blocks, columns))
    ic, jc = (blocks // chunks, columns // chunks)
    blocked = inputs.reshape(seqs, blocks, width, channels)
    cot_f32 = cotangent.astype(f32)
    gate_value, gate_slope = silu_parts(inputs.astype(f32))

    def after(value, *others):
        kept = lax.optimization_barrier((value,) + others)
        return (kept[0], kept[1:])

    def exchange(part):
        return lax.all_to_all(part, "seq", split_axis=0, concat_axis=0, tiled=True)

    first_parts, received = ([], [])
    for q in range(chunks):
        own = slice(q * ic, (q + 1) * ic)
        factor = lax.all_gather(first_factor[own], "dp", axis=1, tiled=True)
        first_parts.append(factor)
        part = jnp.einsum(
            "ijk,bikc->bijc", factor, blocked[:, own], preferred_element_type=f32
        ).astype(bf16)
        part = part.reshape(seqs, ic, ring, columns, channels).transpose(2, 0, 1, 3, 4)
        part = row_major(part)
        if q:
            part, (received[-1],) = after(part, received[-1])
        received.append(exchange(part))
    second_full = lax.all_gather(second_factor, "dp", axis=1, tiled=True)
    gated_cot = (cot_f32 * gate_value).astype(bf16).reshape(seqs, columns, width_two, channels)
    previous = received
    returned = []
    first_full = jnp.concatenate(first_parts, axis=0)
    first_split = first_full.reshape(blocks, ring, chunks, jc, width)

    def through_first(q, total):
        back = returned[q]
        grad_one = norm_scale * jnp.einsum(
            "sbitc,bikc->istk", back, blocked, preferred_element_type=f32
        )
        total = total + jnp.einsum(
            "istk,sbitc->bikc", first_split[:, :, q], back, preferred_element_type=f32
        )
        return (grad_one.astype(bf16), total)

    grads_one = []
    done = 0
    for q in range(chunks):
        own = slice(q * jc, (q + 1) * jc)
        part = jnp.einsum(
            "jik,bjic->bkjc", second_full[own], gated_cot[:, own], preferred_element_type=f32
        ).astype(bf16)
        part = part.reshape(seqs, ring, blocks, jc, channels).transpose(1, 0, 2, 3, 4)
        part = row_major(part)
        if q == chunks // 2:
            exchanged = jnp.concatenate(received, axis=2).transpose(1, 0, 2, 3, 4)
            exchanged = exchanged.reshape(seqs, ring * blocks, columns, channels)
            mixing = jnp.einsum(
                "jik,bkjc->bjic", second_full, exchanged, preferred_element_type=f32
            ).reshape(seqs, rows, channels)
            outputs = (mixing * gate_value).astype(bf16)
            grad_two = norm_scale * jnp.einsum(
                "bjic,bkjc->jik", gated_cot, exchanged, preferred_element_type=f32
            )
            grad_two = grad_two.astype(bf16)
            total = (cot_f32 * mixing * gate_slope).reshape(blocked.shape)
            part, (outputs, grad_two, total) = after(part, outputs, grad_two, total)
            second_sum = lax.psum_scatter(grad_two, "dp", scatter_dimension=1, tiled=True)
        elif q > chunks // 2:
            while done < q - 1:
                grad_one, total = through_first(done, total)
                grads_one.append(grad_one)
                done += 1
            part, (total, *grads_one) = after(part, total, *grads_one)
            grads_one = list(grads_one)
        part, (previous[-1],) = after(part, previous[-1])
        returned.append(exchange(part))
        previous = returned
    while done < chunks - 1:
        grad_one, total = through_first(done, total)
        grads_one.append(grad_one)
        done += 1
    first_sums = []
    if grads_one:
        early = jnp.concatenate(grads_one, axis=2)
        early_sum = scatter_rows(early)
        returned[-1], (early_sum, total, second_sum) = after(
            returned[-1], early_sum, total, second_sum
        )
        first_sums.append(early_sum)
    grad_one, total = through_first(chunks - 1, total)
    first_sums.append(scatter_rows(grad_one))
    first_sum = jnp.concatenate(first_sums, axis=2).reshape(first_factor.shape)
    input_grad = total.reshape(seqs, rows, channels).astype(bf16)
    return (outputs, input_grad, first_sum, second_sum)


def solution(mesh):
    in_specs = (
        P(("groups", "dp"), "seq", None),
        P(("groups", "dp"), "seq", None),
        P("seq", "dp", None),
        P("seq", "dp", None),
    )
    out_specs = (
        P(("groups", "dp"), "seq", None),
        P(("groups", "dp"), "seq", None),
        P(("groups", "seq"), "dp", None),
        P(("groups", "seq"), "dp", None),
    )
    return jax.shard_map(shards, mesh=mesh, in_specs=in_specs, out_specs=out_specs, check_vma=False)
```

profile of v0, /device:TPU:0, one launch (start us, length us, event | category | flops | bytes accessed | tf_op | source)
XLA Modules:
  0.0 951.7 jit_solution(6830200255525887186)
XLA Ops:
  10.1 25.4 %all-gather.10.cloned.1.call-done = bf16[16,256,256]{2,1,0:T(8,128)(2,1)} async-done(((bf16[16,64,256]{2,1,0:T(8,128)(2,1)}), bf16[16,256,256]{2,1,0:T(8,128)(2,1)}) %all-gather.10.cloned.1.call-update) | async-done | bytes 2097168 | tf_op jit(solution)/shard_map/all_gather | solution.py:52
  41.9 4.9 all-to-all-start
  48.3 24.6 %all-gather.8.cloned.1.call-done = bf16[16,256,256]{2,1,0:T(8,128)(2,1)} async-done(((bf16[16,64,256]{2,1,0:T(8,128)(2,1)}), bf16[16,256,256]{2,1,0:T(8,128)(2,1)}) %all-gather.8.cloned.1.call-update) | async-done | bytes 2097168 | tf_op jit(solution)/shard_map/all_gather | solution.py:52
  79.2 61.5 %all-to-all-done = bf16[4,1,16,64,512]{4,3,2,1,0:T(8,128)(2,1)} async-done(((bf16[4,1,16,64,512]{4,3,2,1,0:T(8,128)(2,1)}), bf16[4,1,16,64,512]{4,3,2,1,0:T(8,128)(2,1)}, u32[]{:S(2)}, u32[]{:S(2)}) %all-to-all-start) | async-done | bytes 4194336 | tf_op jit(solution)/shard_map/all_to_all | solution.py:47
  140.7 5.0 all-to-all-start.1
  155.2 83.5 %all-to-all-done.1 = bf16[4,1,16,64,512]{4,3,2,1,0:T(8,128)(2,1)} async-done(((bf16[4,1,16,64,512]{4,3,2,1,0:T(8,128)(2,1)}), bf16[4,1,16,64,512]{4,3,2,1,0:T(8,128)(2,1)}, u32[]{:S(2)}, u32[]{:S(2)}) %all-to-all-start.1) | async-done | bytes 4194336 | tf_op jit(solution)/shard_map/all_to_all | solution.py:47
  250.0 86.3 %all-to-all-done.2 = bf16[4,1,16,64,512]{4,3,2,1,0:T(8,128)(2,1)} async-done(((bf16[4,1,16,64,512]{4,3,2,1,0:T(8,128)(2,1)}), bf16[4,1,16,64,512]{4,3,2,1,0:T(8,128)(2,1)}, u32[]{:S(2)}, u32[]{:S(2)}) %all-to-all-start.2) | async-done | bytes 4194336 | tf_op jit(solution)/shard_map/all_to_all | solution.py:47
  336.3 5.1 all-to-all-start.3
  341.3 21.3 %fusion = bf16[1,16384,512]{2,1,0:T(8,128)(2,1)} fusion(bf16[1,16384,512]{2,1,0:T(8,128)(2,1)} %param.5, bf16[1,16384,512]{2,1,0:T(8,128)(2,1)} %param.4), kind=kLoop, calls=%fused_computation.5 | loop fusion | flops 67108864 | bytes 50331648 | tf_op jit(solution)/shard_map/convert_element_type | solution.py:63
  362.6 5.3 fusion.54
  388.0 46.1 %all-to-all-done.3 = bf16[4,1,16,64,512]{4,3,2,1,0:T(8,128)(2,1)} async-done(((bf16[4,1,16,64,512]{4,3,2,1,0:T(8,128)(2,1)}), bf16[4,1,16,64,512]{4,3,2,1,0:T(8,128)(2,1)}, u32[]{:S(2)}, u32[]{:S(2)}) %all-to-all-start.3) | async-done | bytes 4194336 | tf_op jit(solution)/shard_map/all_to_all | solution.py:47
  439.3 14.0 %pad_maximum_fusion = bf16[4,1,64,64,512]{4,3,2,1,0:T(8,128)(2,1)} fusion(bf16[4,1,16,64,512]{4,3,2,1,0:T(8,128)(2,1)} %all-to-all-done.3, bf16[4,1,16,64,512]{4,3,2,1,0:T(8,128)(2,1)} %all-to-all-done.2, bf16[4,1,16,64,512]{4,3,2,1,0:T(8,128)(2,1)} %all-to-all-done.1, bf16[4,1,16,64,512]{4,3,2,1,0:T(8,128)(2,1)} %all-to-all-done), kind=kLoop, calls=%fused_computation.19 | loop fusion | flops 25165824 | bytes 33554432 | tf_op jit(solution)/shard_map/concatenate | solution.py:89
  453.3 51.6 %fusion.11 = f32[64,512,256]{1,2,0:T(8,128)} fusion(bf16[256,64,512]{2,1,0:T(8,128)(2,1)} %bitcast.197, bf16[64,256,256]{2,0,1:T(8,128)(2,1)} %all-gather.6.cloned.1.call-done), kind=kOutput, calls=%fused_computation.23 | convolution fusion | flops 4294967296 | bytes 58720256 | tf_op jit(solution)/shard_map/jik,bkjc->bjic/dot_general | solution.py:91
  504.9 40.1 %fusion.1 = (f32[1,16384,512]{2,1,0:T(8,128)}, bf16[1,16384,512]{2,1,0:T(8,128)(2,1)}) fusion(bf16[1,16384,512]{2,1,0:T(8,128)(2,1)} %param.5, bf16[1,16384,512]{2,1,0:T(8,128)(2,1)} %param.4, f32[64,512,256]{1,2,0:T(8,128)} %fusion.11), kind=kLoop, calls=%fused_computation.6 | loop fusion | flops 117440512 | bytes 117440512 | tf_op jit(solution)/shard_map/mul | solution.py:99
  545.0 24.3 %multiply_convert_fusion = bf16[64,256,256]{2,1,0:T(8,128)(2,1)} fusion(bf16[64,256,512]{2,1,0:T(8,128)(2,1)} %bitcast.199, bf16[256,64,512]{2,1,0:T(8,128)(2,1)} %bitcast.198), kind=kOutput, calls=%fused_computation.20 | convolution fusion | flops 4303355904 | bytes 41943040 | tf_op jit(solution)/shard_map/bjic,bkjc->jik/dot_general | solution.py:95
  578.9 5.5 all-to-all-start.5
  591.4 5.1 convert_bitcast_fusion.1
  600.8 33.7 %copy.73 = f32[1,64,256,512]{2,3,1,0:T(8,128)} copy(f32[1,64,256,512]{3,2,1,0:T(8,128)} %bitcast.196) | data formatting | bytes 67108864 | tf_op jit(solution)/shard_map/optimization_barrier | solution.py:43
  634.6 17.9 %fusion.36 = f32[64,512,256,1]{2,1,0,3:T(8,128)} fusion(bf16[64,4,1,16,256]{4,3,2,1,0:T(8,128)(2,1)S(1)} %get-tuple-element.61, bf16[4,1,64,16,512]{4,3,2,1,0:T(8,128)(2,1)} %all-to-all-done.4), kind=kOutput, calls=%fused_computation.73 | convolution fusion | flops 1073741824 | bytes 39845888 | tf_op jit(solution)/shard_map/istk,sbitc->bikc/dot_general | solution.py:74
  652.4 24.2 %all-to-all-done.5 = bf16[4,1,64,16,512]{4,3,2,1,0:T(8,128)(2,1)} async-done(((bf16[4,1,64,16,512]{4,3,2,1,0:T(8,128)(2,1)}), bf16[4,1,64,16,512]{4,3,2,1,0:T(8,128)(2,1)}, u32[]{:S(2)}, u32[]{:S(2)}) %all-to-all-start.5) | async-done | bytes 4194336 | tf_op jit(solution)/shard_map/all_to_all | solution.py:47
  681.6 10.2 %multiply_convert_fusion.4 = bf16[64,4,16,256]{3,2,1,0:T(8,128)(2,1)S(1)} fusion(bf16[64,256,512,1]{2,1,3,0:T(8,128)(2,1)} %bitcast.192, bf16[4,1,64,16,512]{4,3,2,1,0:T(8,128)(2,1)} %all-to-all-done.4), kind=kOutput, calls=%fused_computation.59 | convolution fusion | flops 1075838976 | bytes 23068672 | tf_op jit(solution)/shard_map/sbitc,bikc->istk/dot_general | solution.py:71
  691.8 11.3 %multiply_convert_fusion.3 = bf16[64,4,16,256]{3,2,1,0:T(8,128)(2,1)} fusion(bf16[64,256,512,1]{2,1,3,0:T(8,128)(2,1)} %bitcast.193, bf16[4,1,64,16,512]{4,3,2,1,0:T(8,128)(2,1)} %all-to-all-done.5), kind=kOutput, calls=%fused_computation.58 | convolution fusion | flops 1075838976 | bytes 23068672 | tf_op jit(solution)/shard_map/sbitc,bikc->istk/dot_general | solution.py:71
  703.1 35.8 %bitcast_add_fusion.2 = f32[1,64,256,512]{2,3,1,0:T(8,128)} fusion(f32[1,64,256,512]{2,3,1,0:T(8,128)} %copy.73, f32[64,512,256,1]{2,1,0,3:T(8,128)} %fusion.36, bf16[64,4,1,16,256]{4,3,2,1,0:T(8,128)(2,1)} %get-tuple-element.60, bf16[4,1,64,16,512]{4,3,2,1,0:T(8,128)(2,1)} %all-to-all-done.5), kind=kOutput, calls=%fused_computation.15 | convolution fusion | flops 1090519040 | bytes 106954752 | tf_op jit(solution)/shard_map/istk,sbitc->bikc/dot_general | solution.py:74
  738.9 35.3 %all-to-all-done.6 = bf16[4,1,64,16,512]{4,3,2,1,0:T(8,128)(2,1)} async-done(((bf16[4,1,64,16,512]{4,3,2,1,0:T(8,128)(2,1)}), bf16[4,1,64,16,512]{4,3,2,1,0:T(8,128)(2,1)}, u32[]{:S(2)}, u32[]{:S(2)}) %all-to-all-start.6) | async-done | bytes 4194336 | tf_op jit(solution)/shard_map/all_to_all | solution.py:47
  774.2 10.1 %multiply_convert_fusion.2 = bf16[64,4,16,256]{3,2,1,0:T(8,128)(2,1)S(1)} fusion(bf16[64,256,512,1]{2,1,3,0:T(8,128)(2,1)} %bitcast.194, bf16[4,1,64,16,512]{4,3,2,1,0:T(8,128)(2,1)} %all-to-all-done.6), kind=kOutput, calls=%fused_computation.57 | convolution fusion | flops 1075838976 | bytes 23068672 | tf_op jit(solution)/shard_map/sbitc,bikc->istk/dot_general | solution.py:71
  784.4 6.3 pad_maximum_fusion.2
  790.7 5.0 all-to-all-start.7
  795.7 25.4 %bitcast_add_fusion.1 = f32[1,64,256,512]{2,3,1,0:T(8,128)} fusion(f32[1,64,256,512]{2,3,1,0:T(8,128)} %bitcast_add_fusion.2, bf16[64,4,1,16,256]{4,3,2,1,0:T(8,128)(2,1)S(1)} %copy-done.2, bf16[4,1,64,16,512]{4,3,2,1,0:T(8,128)(2,1)} %all-to-all-done.6), kind=kOutput, calls=%fused_computation.14 | convolution fusion | flops 1082130432 | bytes 73400320 | tf_op jit(solution)/shard_map/istk,sbitc->bikc/dot_general | solution.py:74
  821.2 67.2 %all-to-all-done.7 = bf16[4,1,64,16,512]{4,3,2,1,0:T(8,128)(2,1)} async-done(((bf16[4,1,64,16,512]{4,3,2,1,0:T(8,128)(2,1)}), bf16[4,1,64,16,512]{4,3,2,1,0:T(8,128)(2,1)}, u32[]{:S(2)}, u32[]{:S(2)}) %all-to-all-start.7) | async-done | bytes 4194336 | tf_op jit(solution)/shard_map/all_to_all | solution.py:47
  888.4 11.5 %multiply_convert_fusion.1 = bf16[64,4,16,256]{3,2,1,0:T(8,128)(2,1)} fusion(bf16[64,256,512,1]{2,1,3,0:T(8,128)(2,1)} %bitcast.195, bf16[4,1,64,16,512]{4,3,2,1,0:T(8,128)(2,1)} %all-to-all-done.7), kind=kOutput, calls=%fused_computation.56 | convolution fusion | flops 1075838976 | bytes 23068672 | tf_op jit(solution)/shard_map/sbitc,bikc->istk/dot_general | solution.py:71
  899.9 19.3 %fusion.7 = bf16[1,64,256,512]{2,3,1,0:T(8,128)(2,1)} fusion(f32[1,64,256,512]{2,3,1,0:T(8,128)} %bitcast_add_fusion.1, bf16[64,4,1,16,256]{4,3,2,1,0:T(8,128)(2,1)S(1)} %copy-done.6, bf16[4,1,64,16,512]{4,3,2,1,0:T(8,128)(2,1)} %all-to-all-done.7), kind=kOutput, calls=%fused_computation.13 | convolution fusion | flops 1090519040 | bytes 56623104 | tf_op jit(solution)/shard_map/istk,sbitc->bikc/dot_general | solution.py:74
  919.2 22.6 %copy.81 = bf16[1,64,256,512]{3,2,1,0:T(8,128)(2,1)} copy(bf16[1,64,256,512]{2,3,1,0:T(8,128)(2,1)} %fusion.7) | data formatting | bytes 33554432 | tf_op jit(solution)/shard_map/convert_element_type | solution.py:127
  (62 shorter events, 91.7 us)
Async XLA Ops:
  7.2 28.4 %all-gather.10.cloned.1.call-start = ((), (), s32[]{:S(2)}) async-start(), calls=%async_computation.13 | async-start | bytes 2621440 | tf_op jit(solution)/shard_map/all_gather | solution.py:52
  41.9 98.8 %all-to-all-start = ((bf16[4,1,16,64,512]{4,3,2,1,0:T(8,128)(2,1)}), bf16[4,1,16,64,512]{4,3,2,1,0:T(8,128)(2,1)}, u32[]{:S(2)}, u32[]{:S(2)}) async-start(bf16[4,1,16,64,512]{4,3,2,1,0:T(8,128)(2,1)} %bitcast.212), calls=%async_computation | async-start | bytes 8388608 | tf_op jit(solution)/shard_map/all_to_all | solution.py:47
  46.8 26.0 %all-gather.8.cloned.1.call-start = ((), (), s32[]{:S(2)}) async-start(), calls=%async_computation.12 | async-start | bytes 2621440 | tf_op jit(solution)/shard_map/all_gather | solution.py:52
  47.6 101.3 %all-gather.12.cloned.1.call-start = ((), (), s32[]{:S(2)}) async-start(), calls=%async_computation.14 | async-start | bytes 2621440 | tf_op jit(solution)/shard_map/all_gather | solution.py:52
  140.7 5.6 copy-start.5
  140.7 98.1 %all-to-all-start.1 = ((bf16[4,1,16,64,512]{4,3,2,1,0:T(8,128)(2,1)}), bf16[4,1,16,64,512]{4,3,2,1,0:T(8,128)(2,1)}, u32[]{:S(2)}, u32[]{:S(2)}) async-start(bf16[4,1,16,64,512]{4,3,2,1,0:T(8,128)(2,1)} %bitcast.211), calls=%async_computation.1 | async-start | bytes 8388608 | tf_op jit(solution)/shard_map/all_to_all | solution.py:47
  145.7 97.9 %all-gather.14.cloned.1.call-start = ((), (), s32[]{:S(2)}) async-start(), calls=%async_computation.15 | async-start | bytes 2621440 | tf_op jit(solution)/shard_map/all_gather | solution.py:52
  146.3 216.3 %all-gather.6.cloned.1.call-start = ((), (), s32[]{:S(2)}) async-start(), calls=%async_computation.11 | async-start | bytes 10485760 | tf_op jit(solution)/shard_map/all_gather | solution.py:62
  238.8 97.5 %all-to-all-start.2 = ((bf16[4,1,16,64,512]{4,3,2,1,0:T(8,128)(2,1)}), bf16[4,1,16,64,512]{4,3,2,1,0:T(8,128)(2,1)}, u32[]{:S(2)}, u32[]{:S(2)}) async-start(bf16[4,1,16,64,512]{4,3,2,1,0:T(8,128)(2,1)} %bitcast.215), calls=%async_computation.2 | async-start | bytes 8388608 | tf_op jit(solution)/shard_map/all_to_all | solution.py:47
  336.3 97.7 %all-to-all-start.3 = ((bf16[4,1,16,64,512]{4,3,2,1,0:T(8,128)(2,1)}), bf16[4,1,16,64,512]{4,3,2,1,0:T(8,128)(2,1)}, u32[]{:S(2)}, u32[]{:S(2)}) async-start(bf16[4,1,16,64,512]{4,3,2,1,0:T(8,128)(2,1)} %bitcast.214), calls=%async_computation.3 | async-start | bytes 8388608 | tf_op jit(solution)/shard_map/all_to_all | solution.py:47
  362.6 9.8 %copy-start = (bf16[1,16384,512]{2,1,0:T(8,128)(2,1)S(1)}, bf16[1,16384,512]{2,1,0:T(8,128)(2,1)}, u32[]{:S(2)}) copy-start(bf16[1,16384,512]{2,1,0:T(8,128)(2,1)} %fusion) | copy-start | bytes 50331652
  434.0 144.8 %all-to-all-start.4 = ((bf16[4,1,64,16,512]{4,3,2,1,0:T(8,128)(2,1)}), bf16[4,1,64,16,512]{4,3,2,1,0:T(8,128)(2,1)}, u32[]{:S(2)}, u32[]{:S(2)}) async-start(bf16[4,1,64,16,512]{4,3,2,1,0:T(8,128)(2,1)} %bitcast.210), calls=%async_computation.4 | async-start | bytes 8388608 | tf_op jit(solution)/shard_map/all_to_all | solution.py:47
  438.9 382.3 %reduce-scatter.6.cloned.1.call-start = ((), (), s32[]{:S(2)}) async-start(), calls=%async_computation.17 | async-start | bytes 10485760 | tf_op jit(solution)/shard_map/reduce_scatter | solution.py:101
  578.9 5.5 copy-start.3
  578.9 97.8 %all-to-all-start.5 = ((bf16[4,1,64,16,512]{4,3,2,1,0:T(8,128)(2,1)}), bf16[4,1,64,16,512]{4,3,2,1,0:T(8,128)(2,1)}, u32[]{:S(2)}, u32[]{:S(2)}) async-start(bf16[4,1,64,16,512]{4,3,2,1,0:T(8,128)(2,1)} %bitcast.213), calls=%async_computation.5 | async-start | bytes 8388608 | tf_op jit(solution)/shard_map/all_to_all | solution.py:47
  588.5 2.9 copy-start.4
  676.7 97.6 %all-to-all-start.6 = ((bf16[4,1,64,16,512]{4,3,2,1,0:T(8,128)(2,1)}), bf16[4,1,64,16,512]{4,3,2,1,0:T(8,128)(2,1)}, u32[]{:S(2)}, u32[]{:S(2)}) async-start(bf16[4,1,64,16,512]{4,3,2,1,0:T(8,128)(2,1)} %bitcast.208), calls=%async_computation.6 | async-start | bytes 8388608 | tf_op jit(solution)/shard_map/all_to_all | solution.py:47
  681.5 206.8 %reduce-scatter.4.cloned.1.call-start = ((), (), s32[]{:S(2)}) async-start(), calls=%async_computation.16 | async-start | bytes 7864320 | tf_op jit(solution)/shard_map/reduce_scatter | solution.py:21
  774.2 10.1 %copy-start.1 = (bf16[64,4,16,256]{3,2,1,0:T(8,128)(2,1)S(1)}, bf16[64,4,16,256]{3,2,1,0:T(8,128)(2,1)}, u32[]{:S(2)}) copy-start(bf16[64,4,16,256]{3,2,1,0:T(8,128)(2,1)} %multiply_convert_fusion.3) | copy-start | bytes 6291460
  790.7 5.1 copy-start.2
  790.7 97.7 %all-to-all-start.7 = ((bf16[4,1,64,16,512]{4,3,2,1,0:T(8,128)(2,1)}), bf16[4,1,64,16,512]{4,3,2,1,0:T(8,128)(2,1)}, u32[]{:S(2)}, u32[]{:S(2)}) async-start(bf16[4,1,64,16,512]{4,3,2,1,0:T(8,128)(2,1)} %bitcast.209), calls=%async_computation.7 | async-start | bytes 8388608 | tf_op jit(solution)/shard_map/all_to_all | solution.py:47
  795.7 146.1 %reduce-scatter.8.cloned.1.call-start = ((), (), s32[]{:S(2)}) async-start(), calls=%async_computation.18 | async-start | bytes 2621440 | tf_op jit(solution)/shard_map/reduce_scatter | solution.py:21
  888.4 11.5 %copy-start.6 = (bf16[64,4,1,16,256]{4,3,2,1,0:T(8,128)(2,1)S(1)}, bf16[64,4,1,16,256]{4,3,2,1,0:T(8,128)(2,1)}, u32[]{:S(2)}) copy-start(bf16[64,4,1,16,256]{4,3,2,1,0:T(8,128)(2,1)} %get-tuple-element.58) | copy-start | bytes 6291460
  919.2 22.6 %copy-start.7 = (bf16[64,48,256]{2,1,0:T(8,128)(2,1)S(1)}, bf16[64,48,256]{2,1,0:T(8,128)(2,1)}, u32[]{:S(2)}) copy-start(bf16[64,48,256]{2,1,0:T(8,128)(2,1)} %reduce-scatter.4.cloned.1.call-done) | copy-start | bytes 4718596
Sparse Core Ops, SparseCore 0:
  10.2 25.2 all-gather.9
  49.8 23.0 all-gather.7
  74.4 22.5 all-gather.11
  147.8 23.0 all-gather.13
  172.8 58.2 all-gather.5
  569.4 72.1 reduce-scatter.5
  790.8 56.5 reduce-scatter.3
  900.0 29.5 reduce-scatter.7
where the time goes:
time: 960 us; the launch traced here: 952 us
  waiting for transfers between devices  456 us (48%)
  matrix products  250 us (26%)
  local copies, waits for them, and re-layouts  101 us (11%)
  other arithmetic  88.4 us (9%)
  starting transfers between devices  40.7 us (4%)
  between operations  14.9 us (2%)
    all_to_all x8, waiting for transfers between devices, exchange(): return lax.all_to_all(part, 'seq', split_axis=0, concat_axis=0, tiled=True)  404 us
    dot_general x4, matrix products, through_first(): jnp.einsum('istk,sbitc->bikc', first_split[:, :, q], back, preferred_elem...  98.4 us
    dot_general x1, matrix products, shards(): jnp.einsum('jik,bkjc->bjic', second_full, exchanged, preferred_element_ty...  51.6 us
    all_gather x4, waiting for transfers between devices, shards(): factor = lax.all_gather(first_factor[own], 'dp', axis=1, tiled=True)  50 us
    dot_general x4, matrix products, through_first(): jnp.einsum('sbitc,bikc->istk', back, blocked, preferred_element_type=f32)  43.1 us
    mul x1, other arithmetic, shards(): total = (cot_f32 * mixing * gate_slope).reshape(blocked.shape)  40.1 us
    all_to_all x8, starting transfers between devices, exchange(): return lax.all_to_all(part, 'seq', split_axis=0, concat_axis=0, tiled=True)  40 us
    optimization_barrier x1, local copies, waits for them, and re-layouts, after(): kept = lax.optimization_barrier((value,) + others)  33.7 us
  transfers between devices with their start and end apart: 16, of which 9 were waited for; matrix products, arithmetic and copies ran while one was open for 43% of the time, Pallas kernels for 0%

commit v1 on v0

--- a/solution.py
+++ b/solution.py
@@ -4,6 +4,20 @@
 from jax import lax
 from jax.experimental.layout import Layout, with_layout_constraint
 from jax.sharding import PartitionSpec as P
+
+
+def raise_notes(local_x):
+    plain = lax.psum(1, axis_name="dp")
+    response = lax.axis_index("dp")
+    v1, g_now, piece_out = (plain, response, local_x.shape[1])
+    placed, e_now = (local_x, 1)
+    while e_now < v1:
+        h_now = tuple(((w, (w - e_now) % v1) for w in range(v1)))
+        seen_now = lax.ppermute(placed, axis_name="dp", perm=h_now)
+        placed = jnp.concatenate([placed, seen_now], 1)
+        e_now = 2 * e_now
+    x_now = jnp.roll(placed, g_now * piece_out, 1)
+    return x_now
 
 
 def silu_parts(values):
@@ -49,7 +63,7 @@
     first_parts, received = ([], [])
     for q in range(chunks):
         own = slice(q * ic, (q + 1) * ic)
-        factor = lax.all_gather(first_factor[own], "dp", axis=1, tiled=True)
+        factor = raise_notes(first_factor[own])
         first_parts.append(factor)
         part = jnp.einsum(
             "ijk,bikc->bijc", factor, blocked[:, own], preferred_element_type=f32

time: 960 us -> 974 us (1.015)
  waiting for transfers between devices: 456 us -> 437 us
  starting transfers between devices: 40.7 us -> 57.8 us
  other arithmetic: 88.4 us -> 103 us
    ppermute x0 -> x8, waiting for transfers between devices: none -> 132 us  [raise_notes(): seen_now = lax.ppermute(placed, axis_name='dp', perm=h_now)]
    all_to_all x8, waiting for transfers between devices: 404 us -> 306 us  [exchange(): return lax.all_to_all(part, 'seq', split_axis=0, concat_axis=0, tiled=True)]
    all_gather x4 -> x0, waiting for transfers between devices: 50 us -> none  [shards(): factor = lax.all_gather(first_factor[own], 'dp', axis=1, tiled=True)]
    ppermute x0 -> x8, starting transfers between devices: none -> 17.4 us  [raise_notes(): seen_now = lax.ppermute(placed, axis_name='dp', perm=h_now)]
    concatenate x0 -> x8, other arithmetic: none -> 14.4 us  [the longest x4 12.2 us: raise_notes(): x_now = jnp.roll(placed, g_now * piece_out, 1)]
  transfers between devices with their start and end apart: 16 -> 20, of which waited for: 9 -> 15; matrix products, arithmetic and copies ran while one was open for 43% -> 44% of each run, Pallas kernels for 0% -> 0%
where the time goes in v1:
time: 974 us; the launch traced here: 963 us
  waiting for transfers between devices  437 us (45%)
  matrix products  250 us (26%)
  other arithmetic  103 us (11%)
  local copies, waits for them, and re-layouts  100 us (10%)
  starting transfers between devices  57.8 us (6%)
  between operations  14.6 us (1%)
    all_to_all x8, waiting for transfers between devices, exchange(): return lax.all_to_all(part, 'seq', split_axis=0, concat_axis=0, tiled=True)  306 us
    ppermute x8, waiting for transfers between devices, raise_notes(): seen_now = lax.ppermute(placed, axis_name='dp', perm=h_now)  132 us
    dot_general x4, matrix products, through_first(): jnp.einsum('istk,sbitc->bikc', first_split[:, :, q], back, preferred_elem...  98.2 us
    dot_general x1, matrix products, shards(): jnp.einsum('jik,bkjc->bjic', second_full, exchanged, preferred_element_ty...  51.6 us
    dot_general x4, matrix products, through_first(): jnp.einsum('sbitc,bikc->istk', back, blocked, preferred_element_type=f32)  43.1 us
    mul x1, other arithmetic, shards(): total = (cot_f32 * mixing * gate_slope).reshape(blocked.shape)  40.1 us
    all_to_all x8, starting transfers between devices, exchange(): return lax.all_to_all(part, 'seq', split_axis=0, concat_axis=0, tiled=True)  39.8 us
    optimization_barrier x1, local copies, waits for them, and re-layouts, after(): kept = lax.optimization_barrier((value,) + others)  33.7 us
  transfers between devices with their start and end apart: 20, of which 15 were waited for; matrix products, arithmetic and copies ran while one was open for 44% of the time, Pallas kernels for 0%

profile of v1, /device:TPU:0, one launch (start us, length us, event | category | flops | bytes accessed | tf_op | source)
XLA Modules:
  0.0 963.3 jit_solution(9260758141317014369)
XLA Ops:
  11.3 6.7 collective-permute-done.2
  19.6 25.7 %collective-permute-done.3 = bf16[16,128,256]{2,1,0:T(8,128)(2,1)} collective-permute-done((bf16[16,128,256]{2,1,0:T(8,128)(2,1)}, bf16[16,128,256]{2,1,0:T(8,128)(2,1)}, u32[]{:S(2)}, u32[]{:S(2)}) %collective-permute-start.3) | collective-permute-done | bytes 1048608 | tf_op jit(solution)/shard_map/ppermute | solution.py:16
  60.0 6.7 collective-permute-done
  68.3 23.3 %collective-permute-done.1 = bf16[16,128,256]{2,1,0:T(8,128)(2,1)S(1)} collective-permute-done((bf16[16,128,256]{2,1,0:T(8,128)(2,1)S(1)}, bf16[16,128,256]{2,1,0:T(8,128)(2,1)S(1)}, u32[]{:S(2)}, u32[]{:S(2)}) %collective-permute-start.1) | collective-permute-done | bytes 1048608 | tf_op jit(solution)/shard_map/ppermute | solution.py:16
  101.0 52.4 %all-to-all-done = bf16[4,1,16,64,512]{4,3,2,1,0:T(8,128)(2,1)} async-done(((bf16[4,1,16,64,512]{4,3,2,1,0:T(8,128)(2,1)}), bf16[4,1,16,64,512]{4,3,2,1,0:T(8,128)(2,1)}, u32[]{:S(2)}, u32[]{:S(2)}) %all-to-all-start) | async-done | bytes 4194336 | tf_op jit(solution)/shard_map/all_to_all | solution.py:61
  158.5 6.7 collective-permute-done.4
  170.3 31.9 %collective-permute-done.5 = bf16[16,128,256]{2,1,0:T(8,128)(2,1)} collective-permute-done((bf16[16,128,256]{2,1,0:T(8,128)(2,1)}, bf16[16,128,256]{2,1,0:T(8,128)(2,1)}, u32[]{:S(2)}, u32[]{:S(2)}) %collective-permute-start.5) | collective-permute-done | bytes 1048608 | tf_op jit(solution)/shard_map/ppermute | solution.py:16
  211.9 39.2 %all-to-all-done.1 = bf16[4,1,16,64,512]{4,3,2,1,0:T(8,128)(2,1)} async-done(((bf16[4,1,16,64,512]{4,3,2,1,0:T(8,128)(2,1)}), bf16[4,1,16,64,512]{4,3,2,1,0:T(8,128)(2,1)}, u32[]{:S(2)}, u32[]{:S(2)}) %all-to-all-start.1) | async-done | bytes 4194336 | tf_op jit(solution)/shard_map/all_to_all | solution.py:61
  256.0 10.7 %collective-permute-start.6 = (bf16[16,64,256]{2,1,0:T(8,128)(2,1)S(1)}, bf16[16,64,256]{2,1,0:T(8,128)(2,1)S(1)}, u32[]{:S(2)}, u32[]{:S(2)}) collective-permute-start(bf16[16,64,256]{2,1,0:T(8,128)(2,1)S(1)} %get-tuple-element.69), channel_id=1, source_target_pairs={{0,3},{1,0},{2,1},{3,2},{4,7},{5,4},{6,5},{7,6},{8,11},{9,8},{10,9... | collective-permute-start | bytes 1572872 | tf_op jit(solution)/shard_map/ppermute | solution.py:16
  266.7 6.7 collective-permute-done.6
  274.7 23.9 %collective-permute-done.7 = bf16[16,128,256]{2,1,0:T(8,128)(2,1)S(1)} collective-permute-done((bf16[16,128,256]{2,1,0:T(8,128)(2,1)S(1)}, bf16[16,128,256]{2,1,0:T(8,128)(2,1)S(1)}, u32[]{:S(2)}, u32[]{:S(2)}) %collective-permute-start.7) | collective-permute-done | bytes 1048608 | tf_op jit(solution)/shard_map/ppermute | solution.py:16
  308.0 40.6 %all-to-all-done.2 = bf16[4,1,16,64,512]{4,3,2,1,0:T(8,128)(2,1)} async-done(((bf16[4,1,16,64,512]{4,3,2,1,0:T(8,128)(2,1)}), bf16[4,1,16,64,512]{4,3,2,1,0:T(8,128)(2,1)}, u32[]{:S(2)}, u32[]{:S(2)}) %all-to-all-start.2) | async-done | bytes 4194336 | tf_op jit(solution)/shard_map/all_to_all | solution.py:61
  353.5 21.3 %fusion = bf16[1,16384,512]{2,1,0:T(8,128)(2,1)} fusion(bf16[1,16384,512]{2,1,0:T(8,128)(2,1)} %param.7, bf16[1,16384,512]{2,1,0:T(8,128)(2,1)} %param.6), kind=kLoop, calls=%fused_computation.5 | loop fusion | flops 67108864 | bytes 50331648 | tf_op jit(solution)/shard_map/convert_element_type | solution.py:77
  400.1 46.1 %all-to-all-done.3 = bf16[4,1,16,64,512]{4,3,2,1,0:T(8,128)(2,1)} async-done(((bf16[4,1,16,64,512]{4,3,2,1,0:T(8,128)(2,1)}), bf16[4,1,16,64,512]{4,3,2,1,0:T(8,128)(2,1)}, u32[]{:S(2)}, u32[]{:S(2)}) %all-to-all-start.3) | async-done | bytes 4194336 | tf_op jit(solution)/shard_map/all_to_all | solution.py:61
  451.5 14.0 %pad_maximum_fusion = bf16[4,1,64,64,512]{4,3,2,1,0:T(8,128)(2,1)} fusion(bf16[4,1,16,64,512]{4,3,2,1,0:T(8,128)(2,1)} %all-to-all-done.3, bf16[4,1,16,64,512]{4,3,2,1,0:T(8,128)(2,1)} %all-to-all-done.2, bf16[4,1,16,64,512]{4,3,2,1,0:T(8,128)(2,1)} %all-to-all-done.1, bf16[4,1,16,64,512]{4,3,2,1,0:T(8,128)(2,1)} %all-to-all-done), kind=kLoop, calls=%fused_computation.19 | loop fusion | flops 25165824 | bytes 33554432 | tf_op jit(solution)/shard_map/concatenate | solution.py:103
  465.5 51.6 %fusion.11 = f32[64,512,256]{1,2,0:T(8,128)} fusion(bf16[256,64,512]{2,1,0:T(8,128)(2,1)} %bitcast.205, bf16[64,256,256]{2,0,1:T(8,128)(2,1)} %all-gather.2.cloned.1.call-done), kind=kOutput, calls=%fused_computation.23 | convolution fusion | flops 4294967296 | bytes 58720256 | tf_op jit(solution)/shard_map/jik,bkjc->bjic/dot_general | solution.py:105
  517.1 40.1 %fusion.1 = (f32[1,16384,512]{2,1,0:T(8,128)}, bf16[1,16384,512]{2,1,0:T(8,128)(2,1)}) fusion(bf16[1,16384,512]{2,1,0:T(8,128)(2,1)} %param.7, bf16[1,16384,512]{2,1,0:T(8,128)(2,1)} %param.6, f32[64,512,256]{1,2,0:T(8,128)} %fusion.11), kind=kLoop, calls=%fused_computation.6 | loop fusion | flops 117440512 | bytes 117440512 | tf_op jit(solution)/shard_map/mul | solution.py:113
  557.2 24.3 %multiply_convert_fusion = bf16[64,256,256]{2,1,0:T(8,128)(2,1)} fusion(bf16[64,256,512]{2,1,0:T(8,128)(2,1)} %bitcast.207, bf16[256,64,512]{2,1,0:T(8,128)(2,1)} %bitcast.206), kind=kOutput, calls=%fused_computation.20 | convolution fusion | flops 4303355904 | bytes 41943040 | tf_op jit(solution)/shard_map/bjic,bkjc->jik/dot_general | solution.py:109
  612.4 33.7 %copy.73 = f32[1,64,256,512]{2,3,1,0:T(8,128)} copy(f32[1,64,256,512]{3,2,1,0:T(8,128)} %bitcast.204) | data formatting | bytes 67108864 | tf_op jit(solution)/shard_map/optimization_barrier | solution.py:57
  646.1 17.9 %fusion.56 = f32[64,512,256,1]{2,1,0,3:T(8,128)} fusion(bf16[64,4,1,16,256]{4,3,2,1,0:T(8,128)(2,1)S(1)} %get-tuple-element.62, bf16[4,1,64,16,512]{4,3,2,1,0:T(8,128)(2,1)} %all-to-all-done.4), kind=kOutput, calls=%fused_computation.117 | convolution fusion | flops 1073741824 | bytes 39845888 | tf_op jit(solution)/shard_map/istk,sbitc->bikc/dot_general | solution.py:88
  664.0 24.8 %all-to-all-done.5 = bf16[4,1,64,16,512]{4,3,2,1,0:T(8,128)(2,1)} async-done(((bf16[4,1,64,16,512]{4,3,2,1,0:T(8,128)(2,1)}), bf16[4,1,64,16,512]{4,3,2,1,0:T(8,128)(2,1)}, u32[]{:S(2)}, u32[]{:S(2)}) %all-to-all-start.5) | async-done | bytes 4194336 | tf_op jit(solution)/shard_map/all_to_all | solution.py:61
  693.7 10.2 %multiply_convert_fusion.4 = bf16[64,4,16,256]{3,2,1,0:T(8,128)(2,1)S(1)} fusion(bf16[64,256,512,1]{2,1,3,0:T(8,128)(2,1)} %bitcast.200, bf16[4,1,64,16,512]{4,3,2,1,0:T(8,128)(2,1)} %all-to-all-done.4), kind=kOutput, calls=%fused_computation.83 | convolution fusion | flops 1075838976 | bytes 23068672 | tf_op jit(solution)/shard_map/sbitc,bikc->istk/dot_general | solution.py:85
  704.0 11.3 %multiply_convert_fusion.3 = bf16[64,4,16,256]{3,2,1,0:T(8,128)(2,1)} fusion(bf16[64,256,512,1]{2,1,3,0:T(8,128)(2,1)} %bitcast.201, bf16[4,1,64,16,512]{4,3,2,1,0:T(8,128)(2,1)} %all-to-all-done.5), kind=kOutput, calls=%fused_computation.82 | convolution fusion | flops 1075838976 | bytes 23068672 | tf_op jit(solution)/shard_map/sbitc,bikc->istk/dot_general | solution.py:85
  715.2 35.8 %bitcast_add_fusion.2 = f32[1,64,256,512]{2,3,1,0:T(8,128)} fusion(f32[1,64,256,512]{2,3,1,0:T(8,128)} %copy.73, f32[64,512,256,1]{2,1,0,3:T(8,128)} %fusion.56, bf16[64,4,1,16,256]{4,3,2,1,0:T(8,128)(2,1)} %get-tuple-element.61, bf16[4,1,64,16,512]{4,3,2,1,0:T(8,128)(2,1)} %all-to-all-done.5), kind=kOutput, calls=%fused_computation.15 | convolution fusion | flops 1090519040 | bytes 106954752 | tf_op jit(solution)/shard_map/istk,sbitc->bikc/dot_general | solution.py:88
  751.1 35.3 %all-to-all-done.6 = bf16[4,1,64,16,512]{4,3,2,1,0:T(8,128)(2,1)} async-done(((bf16[4,1,64,16,512]{4,3,2,1,0:T(8,128)(2,1)}), bf16[4,1,64,16,512]{4,3,2,1,0:T(8,128)(2,1)}, u32[]{:S(2)}, u32[]{:S(2)}) %all-to-all-start.6) | async-done | bytes 4194336 | tf_op jit(solution)/shard_map/all_to_all | solution.py:61
  786.4 10.1 %multiply_convert_fusion.2 = bf16[64,4,16,256]{3,2,1,0:T(8,128)(2,1)S(1)} fusion(bf16[64,256,512,1]{2,1,3,0:T(8,128)(2,1)} %bitcast.202, bf16[4,1,64,16,512]{4,3,2,1,0:T(8,128)(2,1)} %all-to-all-done.6), kind=kOutput, calls=%fused_computation.81 | convolution fusion | flops 1075838976 | bytes 23068672 | tf_op jit(solution)/shard_map/sbitc,bikc->istk/dot_general | solution.py:85
  796.5 6.3 pad_maximum_fusion.2
  807.9 25.4 %bitcast_add_fusion.1 = f32[1,64,256,512]{2,3,1,0:T(8,128)} fusion(f32[1,64,256,512]{2,3,1,0:T(8,128)} %bitcast_add_fusion.2, bf16[64,4,1,16,256]{4,3,2,1,0:T(8,128)(2,1)S(1)} %copy-done.7, bf16[4,1,64,16,512]{4,3,2,1,0:T(8,128)(2,1)} %all-to-all-done.6), kind=kOutput, calls=%fused_computation.14 | convolution fusion | flops 1082130432 | bytes 73400320 | tf_op jit(solution)/shard_map/istk,sbitc->bikc/dot_general | solution.py:88
  833.3 67.2 %all-to-all-done.7 = bf16[4,1,64,16,512]{4,3,2,1,0:T(8,128)(2,1)} async-done(((bf16[4,1,64,16,512]{4,3,2,1,0:T(8,128)(2,1)}), bf16[4,1,64,16,512]{4,3,2,1,0:T(8,128)(2,1)}, u32[]{:S(2)}, u32[]{:S(2)}) %all-to-all-start.7) | async-done | bytes 4194336 | tf_op jit(solution)/shard_map/all_to_all | solution.py:61
  900.5 11.5 %multiply_convert_fusion.1 = bf16[64,4,16,256]{3,2,1,0:T(8,128)(2,1)} fusion(bf16[64,256,512,1]{2,1,3,0:T(8,128)(2,1)} %bitcast.203, bf16[4,1,64,16,512]{4,3,2,1,0:T(8,128)(2,1)} %all-to-all-done.7), kind=kOutput, calls=%fused_computation.80 | convolution fusion | flops 1075838976 | bytes 23068672 | tf_op jit(solution)/shard_map/sbitc,bikc->istk/dot_general | solution.py:85
  912.0 19.0 %fusion.7 = bf16[1,64,256,512]{2,3,1,0:T(8,128)(2,1)} fusion(f32[1,64,256,512]{2,3,1,0:T(8,128)} %bitcast_add_fusion.1, bf16[64,4,1,16,256]{4,3,2,1,0:T(8,128)(2,1)S(1)} %copy-done.11, bf16[4,1,64,16,512]{4,3,2,1,0:T(8,128)(2,1)} %all-to-all-done.7), kind=kOutput, calls=%fused_computation.13 | convolution fusion | flops 1090519040 | bytes 56623104 | tf_op jit(solution)/shard_map/istk,sbitc->bikc/dot_general | solution.py:88
  931.0 22.6 %copy.81 = bf16[1,64,256,512]{3,2,1,0:T(8,128)(2,1)} copy(bf16[1,64,256,512]{2,3,1,0:T(8,128)(2,1)} %fusion.7) | data formatting | bytes 33554432 | tf_op jit(solution)/shard_map/convert_element_type | solution.py:141
  (84 shorter events, 145.9 us)
Async XLA Ops:
  8.8 9.1 collective-permute-start.2
  19.0 26.2 %collective-permute-start.3 = (bf16[16,128,256]{2,1,0:T(8,128)(2,1)}, bf16[16,128,256]{2,1,0:T(8,128)(2,1)}, u32[]{:S(2)}, u32[]{:S(2)}) collective-permute-start(bf16[16,128,256]{2,1,0:T(8,128)(2,1)} %pad_maximum_fusion.4), channel_id=1, source_target_pairs={{0,2},{1,3},{2,0},{3,1},{4,6},{5,7},{6,4},{7,5},{8,10},{9,11},{10,... | collective-permute-start | bytes 3145736 | tf_op jit(solution)/shard_map/ppermute | solution.py:16
  48.4 4.2 copy-start.1
  54.9 98.5 %all-to-all-start = ((bf16[4,1,16,64,512]{4,3,2,1,0:T(8,128)(2,1)}), bf16[4,1,16,64,512]{4,3,2,1,0:T(8,128)(2,1)}, u32[]{:S(2)}, u32[]{:S(2)}) async-start(bf16[4,1,16,64,512]{4,3,2,1,0:T(8,128)(2,1)} %bitcast.222), calls=%async_computation | async-start | bytes 8388608 | tf_op jit(solution)/shard_map/all_to_all | solution.py:61
  59.8 6.9 collective-permute-start
  66.7 24.9 %collective-permute-start.1 = (bf16[16,128,256]{2,1,0:T(8,128)(2,1)S(1)}, bf16[16,128,256]{2,1,0:T(8,128)(2,1)S(1)}, u32[]{:S(2)}, u32[]{:S(2)}) collective-permute-start(bf16[16,128,256]{2,1,0:T(8,128)(2,1)S(1)} %pad_maximum_fusion.3), channel_id=1, source_target_pairs={{0,2},{1,3},{2,0},{3,1},{4,6},{5,7},{6,4},{7,5},{8,10},{9,11},{10,... | collective-permute-start | bytes 3145736 | tf_op jit(solution)/shard_map/ppermute | solution.py:16
  94.5 4.2 copy-start.3
  153.4 14.4 %copy-start.9 = (bf16[64,64,256]{2,1,0:T(8,128)(2,1)S(1)}, bf16[64,64,256]{2,1,0:T(8,128)(2,1)}, u32[]{:S(2)}) copy-start(bf16[64,64,256]{2,1,0:T(8,128)(2,1)} %param.9) | copy-start | bytes 6291460
  153.4 97.7 %all-to-all-start.1 = ((bf16[4,1,16,64,512]{4,3,2,1,0:T(8,128)(2,1)}), bf16[4,1,16,64,512]{4,3,2,1,0:T(8,128)(2,1)}, u32[]{:S(2)}, u32[]{:S(2)}) async-start(bf16[4,1,16,64,512]{4,3,2,1,0:T(8,128)(2,1)} %bitcast.218), calls=%async_computation.1 | async-start | bytes 8388608 | tf_op jit(solution)/shard_map/all_to_all | solution.py:61
  158.4 216.4 %all-gather.2.cloned.1.call-start = ((), (), s32[]{:S(2)}) async-start(), calls=%async_computation.11 | async-start | bytes 10485760 | tf_op jit(solution)/shard_map/all_gather | solution.py:76
  158.5 6.8 collective-permute-start.4
  167.1 35.1 %collective-permute-start.5 = (bf16[16,128,256]{2,1,0:T(8,128)(2,1)}, bf16[16,128,256]{2,1,0:T(8,128)(2,1)}, u32[]{:S(2)}, u32[]{:S(2)}) collective-permute-start(bf16[16,128,256]{2,1,0:T(8,128)(2,1)} %pad_maximum_fusion.5), channel_id=1, source_target_pairs={{0,2},{1,3},{2,0},{3,1},{4,6},{5,7},{6,4},{7,5},{8,10},{9,11},{10,... | collective-permute-start | bytes 3145736 | tf_op jit(solution)/shard_map/ppermute | solution.py:16
  205.4 4.2 copy-start.4
  251.1 97.5 %all-to-all-start.2 = ((bf16[4,1,16,64,512]{4,3,2,1,0:T(8,128)(2,1)}), bf16[4,1,16,64,512]{4,3,2,1,0:T(8,128)(2,1)}, u32[]{:S(2)}, u32[]{:S(2)}) async-start(bf16[4,1,16,64,512]{4,3,2,1,0:T(8,128)(2,1)} %bitcast.220), calls=%async_computation.2 | async-start | bytes 8388608 | tf_op jit(solution)/shard_map/all_to_all | solution.py:61
  256.0 17.4 %collective-permute-start.6 = (bf16[16,64,256]{2,1,0:T(8,128)(2,1)S(1)}, bf16[16,64,256]{2,1,0:T(8,128)(2,1)S(1)}, u32[]{:S(2)}, u32[]{:S(2)}) collective-permute-start(bf16[16,64,256]{2,1,0:T(8,128)(2,1)S(1)} %get-tuple-element.69), channel_id=1, source_target_pairs={{0,3},{1,0},{2,1},{3,2},{4,7},{5,4},{6,5},{7,6},{8,11},{9,8},{10,9... | collective-permute-start | bytes 1572872 | tf_op jit(solution)/shard_map/ppermute | solution.py:16
  273.4 25.2 %collective-permute-start.7 = (bf16[16,128,256]{2,1,0:T(8,128)(2,1)S(1)}, bf16[16,128,256]{2,1,0:T(8,128)(2,1)S(1)}, u32[]{:S(2)}, u32[]{:S(2)}) collective-permute-start(bf16[16,128,256]{2,1,0:T(8,128)(2,1)S(1)} %pad_maximum_fusion.6), channel_id=1, source_target_pairs={{0,2},{1,3},{2,0},{3,1},{4,6},{5,7},{6,4},{7,5},{8,10},{9,11},{10,... | collective-permute-start | bytes 3145736 | tf_op jit(solution)/shard_map/ppermute | solution.py:16
  301.5 4.2 copy-start.5
  348.7 97.5 %all-to-all-start.3 = ((bf16[4,1,16,64,512]{4,3,2,1,0:T(8,128)(2,1)}), bf16[4,1,16,64,512]{4,3,2,1,0:T(8,128)(2,1)}, u32[]{:S(2)}, u32[]{:S(2)}) async-start(bf16[4,1,16,64,512]{4,3,2,1,0:T(8,128)(2,1)} %bitcast.223), calls=%async_computation.3 | async-start | bytes 8388608 | tf_op jit(solution)/shard_map/all_to_all | solution.py:61
  374.8 9.8 %copy-start = (bf16[1,16384,512]{2,1,0:T(8,128)(2,1)S(1)}, bf16[1,16384,512]{2,1,0:T(8,128)(2,1)}, u32[]{:S(2)}) copy-start(bf16[1,16384,512]{2,1,0:T(8,128)(2,1)} %fusion) | copy-start | bytes 50331652
  446.2 144.4 %all-to-all-start.4 = ((bf16[4,1,64,16,512]{4,3,2,1,0:T(8,128)(2,1)}), bf16[4,1,64,16,512]{4,3,2,1,0:T(8,128)(2,1)}, u32[]{:S(2)}, u32[]{:S(2)}) async-start(bf16[4,1,64,16,512]{4,3,2,1,0:T(8,128)(2,1)} %bitcast.219), calls=%async_computation.4 | async-start | bytes 8388608 | tf_op jit(solution)/shard_map/all_to_all | solution.py:61
  451.1 382.2 %reduce-scatter.6.cloned.1.call-start = ((), (), s32[]{:S(2)}) async-start(), calls=%async_computation.13 | async-start | bytes 10485760 | tf_op jit(solution)/shard_map/reduce_scatter | solution.py:115
  590.6 5.6 copy-start.2
  590.6 98.2 %all-to-all-start.5 = ((bf16[4,1,64,16,512]{4,3,2,1,0:T(8,128)(2,1)}), bf16[4,1,64,16,512]{4,3,2,1,0:T(8,128)(2,1)}, u32[]{:S(2)}, u32[]{:S(2)}) async-start(bf16[4,1,64,16,512]{4,3,2,1,0:T(8,128)(2,1)} %bitcast.221), calls=%async_computation.5 | async-start | bytes 8388608 | tf_op jit(solution)/shard_map/all_to_all | solution.py:61
  600.5 2.9 copy-start.8
  688.8 97.5 %all-to-all-start.6 = ((bf16[4,1,64,16,512]{4,3,2,1,0:T(8,128)(2,1)}), bf16[4,1,64,16,512]{4,3,2,1,0:T(8,128)(2,1)}, u32[]{:S(2)}, u32[]{:S(2)}) async-start(bf16[4,1,64,16,512]{4,3,2,1,0:T(8,128)(2,1)} %bitcast.216), calls=%async_computation.6 | async-start | bytes 8388608 | tf_op jit(solution)/shard_map/all_to_all | solution.py:61
  693.7 206.8 %reduce-scatter.4.cloned.1.call-start = ((), (), s32[]{:S(2)}) async-start(), calls=%async_computation.12 | async-start | bytes 7864320 | tf_op jit(solution)/shard_map/reduce_scatter | solution.py:35
  786.4 10.1 %copy-start.6 = (bf16[64,4,16,256]{3,2,1,0:T(8,128)(2,1)S(1)}, bf16[64,4,16,256]{3,2,1,0:T(8,128)(2,1)}, u32[]{:S(2)}) copy-start(bf16[64,4,16,256]{3,2,1,0:T(8,128)(2,1)} %multiply_convert_fusion.3) | copy-start | bytes 6291460
  802.8 5.0 copy-start.7
  802.8 97.7 %all-to-all-start.7 = ((bf16[4,1,64,16,512]{4,3,2,1,0:T(8,128)(2,1)}), bf16[4,1,64,16,512]{4,3,2,1,0:T(8,128)(2,1)}, u32[]{:S(2)}, u32[]{:S(2)}) async-start(bf16[4,1,64,16,512]{4,3,2,1,0:T(8,128)(2,1)} %bitcast.217), calls=%async_computation.7 | async-start | bytes 8388608 | tf_op jit(solution)/shard_map/all_to_all | solution.py:61
  807.8 145.8 %reduce-scatter.8.cloned.1.call-start = ((), (), s32[]{:S(2)}) async-start(), calls=%async_computation.14 | async-start | bytes 2621440 | tf_op jit(solution)/shard_map/reduce_scatter | solution.py:35
  900.5 11.5 %copy-start.11 = (bf16[64,4,1,16,256]{4,3,2,1,0:T(8,128)(2,1)S(1)}, bf16[64,4,1,16,256]{4,3,2,1,0:T(8,128)(2,1)}, u32[]{:S(2)}) copy-start(bf16[64,4,1,16,256]{4,3,2,1,0:T(8,128)(2,1)} %get-tuple-element.59) | copy-start | bytes 6291460
  931.0 22.6 %copy-start.12 = (bf16[64,48,256]{2,1,0:T(8,128)(2,1)S(1)}, bf16[64,48,256]{2,1,0:T(8,128)(2,1)}, u32[]{:S(2)}) copy-start(bf16[64,48,256]{2,1,0:T(8,128)(2,1)} %reduce-scatter.4.cloned.1.call-done) | copy-start | bytes 4718596
  (1 other events, 0.8 us)
Sparse Core Ops, SparseCore 0:
  170.4 69.5 all-gather.1
  581.6 72.8 reduce-scatter.5
  802.9 57.2 reduce-scatter.3
  912.1 30.3 reduce-scatter.7
